TPU v7x, 32 devices: a whole 2x2x4 slice. The times are simulated.
32 devices in a mesh: prow: 4 (over z), pcol: 8 (over y, x, core).
Axes of the slice: x: 2, y: 2, z: 4, core: 2. Of those that a mesh axis runs over, the one named last changes fastest.
Arguments:
- window_rhs: float32 [64, 4096], P(None, 'prow'), may hold values from -6 to 6
- past_solution: float32 [64, 16384], P(None, 'pcol'), may hold values from -6 to 6
- past_panel: float32 [4096, 16384], P('prow', 'pcol'), may hold values from -0.046875 to 0.046875
- window_panel: float32 [4, 1024, 8, 1024], P('prow', None, 'pcol'), may hold values from -0.09375 to 0.09375
- diag_inverse: float32 [4, 1024, 1024], P('prow'), may hold values from -1 to 1.5, as said below
- tile_list: int32 [32, 2], P(('prow', 'pcol')), may hold values from 0 to 31
- neighbor_list: int32 [32, 2, 8], P(('prow', 'pcol')), may hold values from 0 to 31
- force_constants: float32 [32, 2, 8, 128, 128], P(('prow', 'pcol')), may hold values from -0.1875 to 0.1875
Outputs:
- solution: float32 [64, 4096], P(None, 'prow')
- residual_forces: float32 [32, 2, 64, 128], P(('prow', 'pcol'))
Inputs may be any that keep to these rules, and one draw needn't show every extreme that they name: `diag_inverse`: each block is lower triangular, with diagonal entries from 0.6 to 1.4.
All inputs are finite; a program needn't handle non-finite values.
Results may differ from a plain program's by a relative error of at most 0.00011.
Values sent between devices are 32-bit elements; how exact they have to be, the bound alone decides.
A program may use at most 128 MiB of HBM per device.

v0:
```python
import jax
import jax.numpy as jnp
from jax import lax
from jax.sharding import PartitionSpec as P


def from_root(block, axis, source):
    block = jnp.where(lax.axis_index(axis) == source, block, jnp.zeros_like(block))
    return lax.psum(block, axis)


def right_product(left, right):
    return lax.dot_general(
        left,
        right,
        (((1,), (1,)), ((), ())),
        precision=lax.Precision.HIGHEST,
        preferred_element_type=jnp.float32,
    )


def per_device(
    window_rhs,
    past_solution,
    past_panel,
    window_panel,
    diag_inverse,
    tile_list,
    neighbor_list,
    force_constants,
):
    row_index = lax.axis_index("prow")
    col_index = lax.axis_index("pcol")
    row_count = lax.axis_size("prow")
    block_order = window_rhs.shape[1]
    full_rhs = lax.all_gather(window_rhs, "prow", axis=1, tiled=True)
    partial_value = right_product(past_solution, past_panel)
    block = window_panel[0, :, 0, :]
    inverse = diag_inverse[0]
    zeros_block = jnp.zeros(window_rhs.shape, jnp.float32)
    solved = []
    for step in range(row_count):
        total = lax.psum(partial_value, "pcol")
        current = lax.cond(
            row_index == step,
            lambda: right_product(window_rhs - total, inverse),
            lambda: zeros_block,
        )
        current = from_root(current, "prow", step)
        partial_value = lax.cond(
            (col_index == step) & (row_index > step),
            lambda: partial_value + right_product(current, block),
            lambda: partial_value,
        )
        solved.append(current)
    whole_solution = jnp.concatenate(solved, axis=1)
    solution = lax.dynamic_slice_in_dim(whole_solution, row_index * block_order, block_order, 1)
    tile_width = force_constants.shape[-1]
    rhs_count = window_rhs.shape[0]
    tiles = whole_solution.reshape(rhs_count, -1, tile_width)
    rhs_tiles = full_rhs.reshape(rhs_count, -1, tile_width)
    near = tiles[:, neighbor_list[0]]
    term = jnp.einsum("rtnb,tnab->tra", near, force_constants[0], precision=lax.Precision.HIGHEST)
    own = jnp.transpose(rhs_tiles[:, tile_list[0]], (1, 0, 2))
    residual_forces = (own - term)[None]
    return (solution, residual_forces)


def solution(mesh):
    placed = (
        P(None, "prow"),
        P(None, "pcol"),
        P("prow", "pcol"),
        P("prow", None, "pcol", None),
        P("prow", None, None),
        P(("prow", "pcol"), None),
        P(("prow", "pcol"), None, None),
        P(("prow", "pcol"), None, None, None, None),
    )
    return jax.shard_map(
        per_device,
        mesh=mesh,
        in_specs=placed,
        out_specs=(P(None, "prow"), P(("prow", "pcol"), None, None, None)),
        check_vma=False,
    )
```

profile of v0, /device:TPU:0, one launch (start us, length us, event | category | flops | bytes accessed | tf_op | source)
XLA Modules:
  0.0 454.1 jit_solution(14231592472993391988)
XLA Ops:
  7.2 12.3 %fusion.12 = f32[64,1024]{1,0:T(8,128)} fusion(f32[64,2048]{1,0:T(8,128)} %param.23, f32[1024,2048]{1,0:T(8,128)} %param.24), kind=kOutput, calls=%fused_computation.34 | convolution fusion | flops 1610612736 | bytes 9175040 | tf_op jit(solution)/shard_map/dot_general | solution.py:13
  19.7 56.3 %all-reduce.9.cloned.1.call-done = f32[64,1024]{1,0:T(8,128)} async-done(((f32[64,1024]{1,0:T(8,128)}), f32[64,1024]{1,0:T(8,128)}) %all-reduce.9.cloned.1.call-update) | async-done | bytes 262160 | tf_op jit(solution)/shard_map/psum | solution.py:43
  76.0 6.3 %conditional.7 = (f32[64,1024]{1,0:T(8,128)S(1)}) conditional(s32[]{:T(128)} %convert_element_type.21, () %tuple.50, (f32[64,1024]{1,0:T(8,128)S(1)}, f32[64,1024]{1,0:T(8,128)}, f32[1024,1024]{1,0:T(8,128)}) %tuple.104), branch_computations={%region_1.0_spmd, %region_2.0_spmd} | conditional | flops 805371904 | bytes 4980744 | solution.py:44
  76.0 6.3 %fusion = f32[64,1024]{1,0:T(8,128)S(1)} fusion(f32[1024,1024]{1,0:T(8,128)} %get-tuple-element.64, f32[64,1024]{1,0:T(8,128)S(1)} %get-tuple-element.62, f32[64,1024]{1,0:T(8,128)} %get-tuple-element.63), kind=kOutput, calls=%fused_computation.2 | convolution fusion | flops 805371904 | bytes 4980736 | tf_op jit(solution)/shard_map/cond/branch_1_fun/dot_general | solution.py:13
  82.3 0.7 broadcast_select_fusion.3
  83.1 0.0 all-reduce.13.cloned.1.call-start
  83.2 5.2 %copy.20 = f32[1,1024,1,1024]{3,1,2,0:T(8,128)} copy(f32[1,1024,1,1024]{3,2,1,0:T(1,128)} %param.25) | data formatting | bytes 8388608
  88.4 26.8 %all-reduce.11.cloned.1.call-done = f32[64,1024]{1,0:T(8,128)} async-done(((f32[64,1024]{1,0:T(8,128)}), f32[64,1024]{1,0:T(8,128)}) %all-reduce.11.cloned.1.call-update) | async-done | bytes 262160 | tf_op jit(solution)/shard_map/psum | solution.py:9
  115.1 0.7 copy-done.2
  115.9 58.1 %all-reduce.13.cloned.1.call-done = f32[64,1024]{1,0:T(8,128)} async-done(((f32[64,1024]{1,0:T(8,128)}), f32[64,1024]{1,0:T(8,128)}) %all-reduce.13.cloned.1.call-update) | async-done | bytes 262160 | tf_op jit(solution)/shard_map/psum | solution.py:43
  174.0 0.7 broadcast_select_fusion.2
  174.9 39.2 %all-reduce.15.cloned.1.call-done = f32[64,1024]{1,0:T(8,128)} async-done(((f32[64,1024]{1,0:T(8,128)}), f32[64,1024]{1,0:T(8,128)}) %all-reduce.15.cloned.1.call-update) | async-done | bytes 262160 | tf_op jit(solution)/shard_map/psum | solution.py:9
  214.1 0.7 copy-done.4
  214.9 56.0 %all-reduce.17.cloned.1.call-done = f32[64,1024]{1,0:T(8,128)} async-done(((f32[64,1024]{1,0:T(8,128)}), f32[64,1024]{1,0:T(8,128)}) %all-reduce.17.cloned.1.call-update) | async-done | bytes 262160 | tf_op jit(solution)/shard_map/psum | solution.py:43
  270.9 0.2 conditional.11
  271.1 0.7 broadcast_select_fusion.1
  272.0 40.0 %all-reduce.19.cloned.1.call-done = f32[64,1024]{1,0:T(8,128)} async-done(((f32[64,1024]{1,0:T(8,128)}), f32[64,1024]{1,0:T(8,128)}) %all-reduce.19.cloned.1.call-update) | async-done | bytes 262160 | tf_op jit(solution)/shard_map/psum | solution.py:9
  312.0 0.7 copy-done.6
  312.7 58.8 %all-reduce.21.cloned.1.call-done = f32[64,1024]{1,0:T(8,128)} async-done(((f32[64,1024]{1,0:T(8,128)}), f32[64,1024]{1,0:T(8,128)}) %all-reduce.21.cloned.1.call-update) | async-done | bytes 262160 | tf_op jit(solution)/shard_map/psum | solution.py:43
  371.6 0.7 broadcast_select_fusion
  372.3 0.0 all-gather.2.cloned.1.call-start
  372.4 0.7 all-gather.2.cloned.1.call-update
  373.1 0.1 reshape.78
  373.3 40.2 %all-reduce.23.cloned.1.call-done = f32[64,1024]{1,0:T(8,128)} async-done(((f32[64,1024]{1,0:T(8,128)}), f32[64,1024]{1,0:T(8,128)}) %all-reduce.23.cloned.1.call-update) | async-done | bytes 262160 | tf_op jit(solution)/shard_map/psum | solution.py:9
  413.5 1.0 constant_dynamic-update-slice_fusion
  414.4 0.1 copy_bitcast_fusion.1
  414.6 1.4 gather_fusion.1
  416.0 0.7 constant_dynamic-slice_fusion
  416.7 26.1 %all-gather.2.cloned.1.call-done = f32[64,4096]{1,0:T(8,128)} async-done(((f32[64,1024]{1,0:T(8,128)}), f32[64,4096]{1,0:T(8,128)}) %all-gather.2.cloned.1.call-update) | async-done | bytes 1048592 | tf_op jit(solution)/shard_map/all_gather | solution.py:36
  442.7 1.3 copy_bitcast_fusion.2
  444.1 0.6 gather_fusion
  444.7 2.9 fusion.9
  (53 shorter events, 0.6 us)
Async XLA Ops:
  7.2 437.5 %copy-start = (f32[1,2,8,128,128]{4,3,2,1,0:T(8,128)S(1)}, f32[1,2,8,128,128]{4,3,2,1,0:T(8,128)}, u32[]{:S(2)}) copy-start(f32[1,2,8,128,128]{4,3,2,1,0:T(8,128)} %param.29) | copy-start | bytes 3145732
  7.2 68.8 %copy-start.7 = (f32[64,1024]{1,0:T(8,128)S(1)}, f32[64,1024]{1,0:T(8,128)}, u32[]{:S(2)}) copy-start(f32[64,1024]{1,0:T(8,128)} %param.22) | copy-start | bytes 786436
  7.2 68.8 %all-reduce.9.cloned.1.call-start = ((), (), s32[]{:S(2)}) async-start(), calls=%async_computation | async-start | bytes 524288 | tf_op jit(solution)/shard_map/psum | solution.py:43
  19.6 95.5 %all-reduce.11.cloned.1.call-start = ((), (), s32[]{:S(2)}) async-start(), calls=%async_computation.1 | async-start | bytes 524288 | tf_op jit(solution)/shard_map/psum | solution.py:9
  83.1 90.9 %all-reduce.13.cloned.1.call-start = ((), (), s32[]{:S(2)}) async-start(), calls=%async_computation.2 | async-start | bytes 524288 | tf_op jit(solution)/shard_map/psum | solution.py:43
  83.1 32.0 %copy-start.1 = (f32[64,1024]{1,0:T(8,128)S(1)}, f32[64,1024]{1,0:T(8,128)}, u32[]{:S(2)}) copy-start(f32[64,1024]{1,0:T(8,128)} %fusion.12) | copy-start | bytes 786436
  115.1 0.7 copy-start.2
  115.9 98.2 %copy-start.3 = (f32[64,1024]{1,0:T(8,128)S(1)}, f32[64,1024]{1,0:T(8,128)}, u32[]{:S(2)}) copy-start(f32[64,1024]{1,0:T(8,128)} %copy-done.2) | copy-start | bytes 786436
  115.9 98.2 %all-reduce.15.cloned.1.call-start = ((), (), s32[]{:S(2)}) async-start(), calls=%async_computation.3 | async-start | bytes 524288 | tf_op jit(solution)/shard_map/psum | solution.py:9
  174.8 96.1 %all-reduce.17.cloned.1.call-start = ((), (), s32[]{:S(2)}) async-start(), calls=%async_computation.4 | async-start | bytes 524288 | tf_op jit(solution)/shard_map/psum | solution.py:43
  214.1 0.7 copy-start.4
  214.8 97.1 %copy-start.5 = (f32[64,1024]{1,0:T(8,128)S(1)}, f32[64,1024]{1,0:T(8,128)}, u32[]{:S(2)}) copy-start(f32[64,1024]{1,0:T(8,128)} %copy-done.4) | copy-start | bytes 786436
  214.8 97.1 %all-reduce.19.cloned.1.call-start = ((), (), s32[]{:S(2)}) async-start(), calls=%async_computation.5 | async-start | bytes 524288 | tf_op jit(solution)/shard_map/psum | solution.py:9
  271.9 99.6 %all-reduce.21.cloned.1.call-start = ((), (), s32[]{:S(2)}) async-start(), calls=%async_computation.6 | async-start | bytes 524288 | tf_op jit(solution)/shard_map/psum | solution.py:43
  311.9 0.7 copy-start.6
  311.9 61.1 %copy-start.11 = (s32[1,2,8]{2,1,0:T(2,128)S(1)}, s32[1,2,8]{2,1,0:T(2,128)}, u32[]{:S(2)}) copy-start(s32[1,2,8]{2,1,0:T(2,128)} %param.28) | copy-start | bytes 196
  311.9 61.2 %copy-start.12 = (s32[1,2]{1,0:T(1,128)S(1)}, s32[1,2]{1,0:T(1,128)}, u32[]{:S(2)}) copy-start(s32[1,2]{1,0:T(1,128)} %param.27) | copy-start | bytes 28
  311.9 61.3 %copy-start.8 = (f32[64,1024]{1,0:T(8,128)S(1)}, f32[64,1024]{1,0:T(8,128)}, u32[]{:S(2)}) copy-start(f32[64,1024]{1,0:T(8,128)} %all-reduce.11.cloned.1.call-done) | copy-start | bytes 786436
  311.9 61.3 %copy-start.9 = (f32[64,1024]{1,0:T(8,128)S(1)}, f32[64,1024]{1,0:T(8,128)}, u32[]{:S(2)}) copy-start(f32[64,1024]{1,0:T(8,128)} %all-reduce.15.cloned.1.call-done) | copy-start | bytes 786436
  312.0 61.3 %copy-start.10 = (f32[64,1024]{1,0:T(8,128)S(1)}, f32[64,1024]{1,0:T(8,128)}, u32[]{:S(2)}) copy-start(f32[64,1024]{1,0:T(8,128)} %all-reduce.19.cloned.1.call-done) | copy-start | bytes 786436
  312.6 100.8 %all-reduce.23.cloned.1.call-start = ((), (), s32[]{:S(2)}) async-start(), calls=%async_computation.7 | async-start | bytes 524288 | tf_op jit(solution)/shard_map/psum | solution.py:9
  372.3 70.4 %all-gather.2.cloned.1.call-start = ((), (), s32[]{:S(2)}) async-start(), calls=%async_computation.8 | async-start | bytes 1310720 | tf_op jit(solution)/shard_map/all_gather | solution.py:36
Sparse Core Ops, SparseCore 0:
  19.7 56.1 all-reduce.8
  83.2 31.8 all-reduce.10
  118.8 55.1 all-reduce.12
  176.3 37.7 all-reduce.14
  217.6 53.2 all-reduce.16
  273.2 38.6 all-reduce.18
  315.5 55.9 all-reduce.20
  374.6 38.8 all-reduce.22
  415.0 27.6 all-gather.1
where the time goes:
time: 454 us
  waiting for transfers between devices  402 us (89%)
  matrix products  21.6 us (5%)
  between operations  14.1 us (3%)
  local copies, waits for them, and re-layouts  12.6 us (3%)
    psum x4, waiting for transfers between devices, per_device(): total = lax.psum(partial_value, 'pcol')  229 us
    psum x4, waiting for transfers between devices, from_root(): return lax.psum(block, axis)  146 us
    all_gather x1, waiting for transfers between devices, per_device(): full_rhs = lax.all_gather(window_rhs, 'prow', axis=1, tiled=True)  26.1 us
    dot_general x2, matrix products, right_product(): lax.dot_general(left, right, (((1,), (1,)), ((), ())), precision=lax.Prec...  18.7 us
  transfers between devices with their start and end apart: 9, of which 9 were waited for; matrix products, arithmetic and copies ran while one was open for 2% of the time, Pallas kernels for 0%

commit v1 on v0

v1 whole, which is shorter than its diff:
```python
import functools

import jax
import jax.numpy as jnp
from jax import lax
from jax.experimental import pallas as pl
from jax.experimental.pallas import tpu as pltpu
from jax.sharding import PartitionSpec as P

MESH = pl.DeviceIdType.MESH
BF16 = jnp.bfloat16
F32 = jnp.float32


def halves(value):
    high = value.astype(BF16)
    return high, (value - high.astype(F32)).astype(BF16)


def nt(left, right):
    return lax.dot_general(left, right, (((1,), (1,)), ((), ())), preferred_element_type=F32)


def nn(left, right):
    return lax.dot_general(left, right, (((1,), (0,)), ((), ())), preferred_element_type=F32)


def kernel(
    rows, cols, owners, tile, nrhs, tpd, nnb,
    rhs_hbm, psol_hbm, panel_hbm, win_hbm, dinv_hbm, tlist, nlist, force_hbm,
    sol_out, res_out,
    psol, panel, win, dinv, force, xpast, xx, whi, wlo, mhi, mlo, fhi, flo,
    part, rs_buf, diff, ubuf, vout, vbuf, y_all, rhs_all,
    load_sem, panel_sem, rhs_sem,
    rs_send, rs_recv, df_send, df_recv, sc_send, ln_send, ag_send, y_recv,
    rl_send, ra_send, r_recv, v_send, v_recv,
):
    p = lax.axis_index("prow")
    q = lax.axis_index("pcol")
    order = owners * tile
    owner = q < owners
    mine = lax.rem(q, owners)
    barrier = pltpu.get_barrier_semaphore()

    def at_plane(step):
        return lax.rem(q + 1 + step, cols)

    def at_line(step):
        return lax.rem(p + 1 + step, rows)

    def remote(src, dst, send, recv, row, col):
        return pltpu.make_async_remote_copy(
            src_ref=src, dst_ref=dst, send_sem=send, recv_sem=recv,
            device_id=(row, col), device_id_type=MESH,
        )

    def act(copy, go):
        if go:
            copy.start()
        else:
            copy.wait_send()

    first = pltpu.make_async_copy(psol_hbm, psol, load_sem.at[0])
    first.start()

    def panel_copy(c):
        at = pl.ds(pl.multiple_of(c * tile, tile), tile)
        return pltpu.make_async_copy(panel_hbm.at[at, :], panel.at[at, :], panel_sem.at[c])

    @pl.loop(0, owners)
    def _(i):
        panel_copy(lax.rem(q + 1 + i, owners)).start()

    def rhs_copy(c):
        return pltpu.make_async_copy(
            rhs_hbm.at[:, c * tile:(c + 1) * tile], rhs_all.at[p * owners + c], rhs_sem.at[c]
        )

    for c in range(owners):
        rhs_copy(c).start()
    load_dinv = pltpu.make_async_copy(dinv_hbm.at[0], dinv, load_sem.at[1])
    load_win = pltpu.make_async_copy(win_hbm.at[0, :, 0, :], win, load_sem.at[2])
    load_force = pltpu.make_async_copy(force_hbm.at[0], force, load_sem.at[3])
    load_dinv.start()
    load_win.start()
    load_force.start()

    @pl.loop(0, cols - 1)
    def _(i):
        pl.semaphore_signal(barrier, inc=1, device_id=(p, at_plane(i)), device_id_type=MESH)

    @pl.loop(0, rows - 1)
    def _(i):
        pl.semaphore_signal(barrier, inc=1, device_id=(at_line(i), q), device_id_type=MESH)

    first.wait()
    high, low = halves(psol[...])
    xpast[0:nrhs, :] = high
    xpast[nrhs:2 * nrhs, :] = low
    for c in range(owners):
        rhs_copy(c).wait()
    pl.semaphore_wait(barrier, cols - 1 + rows - 1)

    def rhs_line(go):
        t = p * owners + mine

        @pl.when(owner)
        def _():
            @pl.loop(0, rows - 1)
            def _(i):
                act(remote(rhs_all.at[t], rhs_all.at[t], rl_send.at[i], r_recv.at[t], at_line(i), q), go)

    rhs_line(True)

    def fold(value):
        turned = value.T
        return turned[:nrhs] + turned[nrhs:]

    def rs_copy(c):
        return remote(part.at[c], rs_buf.at[q], rs_send.at[c], rs_recv.at[q], p, c)

    @pl.loop(0, owners)
    def _(i):
        c = lax.rem(q + 1 + i, owners)
        panel_copy(c).wait()
        high, low = halves(panel[pl.ds(pl.multiple_of(c * tile, tile), tile), :])
        weights = xpast[...]
        part[c] = fold(nt(high, weights) + nt(low, weights))

        @pl.when(c != q)
        def _():
            rs_copy(c).start()

    load_dinv.wait()
    load_win.wait()

    @pl.when(q < p)
    def _():
        step = min(256, order)
        for at in range(0, order, step):
            high, low = halves(win[at:at + step, :])
            whi[at:at + step, :] = high
            wlo[at:at + step, :] = low
        for at in range(0, order, step):
            depth = at + step
            high, low = halves(dinv[at:at + step, :depth])
            value = nn(high, whi[:depth, :]) + nn(low, whi[:depth, :]) + nn(high, wlo[:depth, :])
            high, low = halves(value)
            mhi[at:at + step, :] = high
            mlo[at:at + step, :] = low

    def df_copy(i):
        return remote(diff.at[mine], diff.at[mine], df_send.at[i], df_recv.at[mine], p, at_plane(i))

    def df_all(go):
        @pl.when(owner)
        def _():
            @pl.loop(0, cols - 1)
            def _(i):
                d = at_plane(i)

                @pl.when(((p == 0) & (d < owners)) | (d == p - 1))
                def _():
                    act(df_copy(i), go)

    @pl.when(owner)
    def _():
        @pl.loop(0, cols - 1)
        def _(i):
            s = at_plane(i)
            remote(part.at[mine], rs_buf.at[s], rs_send.at[mine], rs_recv.at[s], p, s).wait_recv()

        total = part[mine]
        for i in range(cols - 1):
            total = total + rs_buf[at_plane(i)]
        diff[mine] = rhs_all[p * owners + mine] - total

    df_all(True)

    def pack(ref, base):
        for c in range(owners):
            high, low = halves(ref[base + c])
            xx[0:nrhs, c * tile:(c + 1) * tile] = high
            xx[nrhs:2 * nrhs, c * tile:(c + 1) * tile] = low

    def solve_tile(c):
        high, low = halves(dinv[pl.ds(pl.multiple_of(c * tile, tile), tile), :])
        weights = xx[...]
        return fold(nt(high, weights) + nt(low, weights))

    def df_wait():
        for c in range(owners):
            @pl.when(c != q)
            def _():
                remote(diff.at[c], diff.at[c], df_send.at[0], df_recv.at[c], p, at_plane(0)).wait_recv()

    def line_send(k, go):
        t = k * owners + mine

        @pl.when(owner)
        def _():
            @pl.loop(0, rows - 1)
            def _(i):
                act(remote(y_all.at[t], y_all.at[t], ln_send.at[i], y_recv.at[t], at_line(i), q), go)

    def plane_send(k, go):
        t = k * owners + mine

        @pl.when(owner)
        def _():
            @pl.loop(0, cols - 1)
            def _(i):
                d = at_plane(i)

                @pl.when((p != k) | (k == 0) | (d != k - 1))
                def _():
                    act(remote(y_all.at[t], y_all.at[t], ag_send.at[k, i], y_recv.at[t], p, d), go)

    def scatter(k, go):
        @pl.loop(0, owners)
        def _(i):
            c = lax.rem(q + 1 + i, owners)
            t = k * owners + c

            @pl.when(c != q)
            def _():
                act(remote(y_all.at[t], y_all.at[t], sc_send.at[c], y_recv.at[t], p, c), go)

    def y_wait(t):
        remote(y_all.at[t], y_all.at[t], ln_send.at[0], y_recv.at[t], p, at_plane(0)).wait_recv()

    def rhs_plane(go):
        @pl.when(owner)
        def _():
            @pl.loop(0, rows - 1)
            def _(j):
                t = at_line(j) * owners + mine
                if go:
                    remote(rhs_all.at[t], rhs_all.at[t], rl_send.at[0], r_recv.at[t], p, at_plane(0)).wait_recv()

                @pl.loop(0, cols - 1)
                def _(i):
                    act(remote(rhs_all.at[t], rhs_all.at[t], ra_send.at[j, i], r_recv.at[t], p, at_plane(i)), go)

    @pl.when(p == 0)
    def _():
        @pl.when(owner)
        def _():
            df_wait()
            pack(diff, 0)
            y_all[mine] = solve_tile(mine)

    @pl.when((p > 0) & (q == p - 1))
    def _():
        df_wait()
        pack(diff, 0)

        @pl.loop(0, owners)
        def _(c):
            ubuf[c] = solve_tile(c)

    def v_copy(j):
        return remote(vout, vbuf.at[j], v_send, v_recv.at[j], p, p - 1)

    load_force.wait()
    for t in range(tpd):
        for n in range(nnb):
            high, low = halves(force[t, n])
            fhi[t, :, n * tile:(n + 1) * tile] = high
            flo[t, :, n * tile:(n + 1) * tile] = low

    @pl.when(p >= 2)
    def _():
        rhs_plane(True)

    for k in range(rows):
        base = k * owners

        @pl.when(owner)
        def _():
            made = (p == k) if k == 0 else ((p == k) & (q == k - 1))

            @pl.when(jnp.logical_not(made))
            def _():
                y_wait(base + mine)

        @pl.when(p == k)
        def _():
            line_send(k, True)

        plane_send(k, True)

        @pl.when((p == k) & (p < 2))
        def _():
            rhs_plane(True)

        @pl.loop(0, cols - 1)
        def _(i):
            c = at_plane(i)

            @pl.when(c < owners)
            def _():
                if k == 0:
                    y_wait(base + c)
                else:
                    @pl.when((p != k) | (q != k - 1))
                    def _():
                        y_wait(base + c)

        if k < rows - 1:
            @pl.when((q == k) & (p > k))
            def _():
                pack(y_all, base)
                weights = xx[...]

                @pl.when(p == k + 1)
                def _():
                    for j in range(k):
                        remote(vout, vbuf.at[j], v_send, v_recv.at[j], p, at_plane(0)).wait_recv()

                    @pl.loop(0, owners)
                    def _(c):
                        at = pl.ds(pl.multiple_of(c * tile, tile), tile)
                        value = ubuf[c] - fold(nt(mhi[at, :], weights) + nt(mlo[at, :], weights))
                        for j in range(k):
                            value = value - vbuf[j, c]
                        y_all[(k + 1) * owners + c] = value

                        @pl.when(c != q)
                        def _():
                            t = (k + 1) * owners + c
                            remote(y_all.at[t], y_all.at[t], sc_send.at[c], y_recv.at[t], p, c).start()

                @pl.when(p > k + 1)
                def _():
                    @pl.loop(0, owners)
                    def _(c):
                        at = pl.ds(pl.multiple_of(c * tile, tile), tile)
                        vout[c] = fold(nt(mhi[at, :], weights) + nt(mlo[at, :], weights))

                    v_copy(k).start()

    for c in range(owners):
        sol_out[:, c * tile:(c + 1) * tile] = y_all[p * owners + c]

    @pl.loop(0, rows - 1)
    def _(j):
        @pl.loop(0, cols - 1)
        def _(i):
            c = at_plane(i)

            @pl.when(c < owners)
            def _():
                t = at_line(j) * owners + c
                remote(rhs_all.at[t], rhs_all.at[t], rl_send.at[0], r_recv.at[t], p, at_plane(0)).wait_recv()

    for t in range(tpd):
        for n in range(nnb):
            high, low = halves(y_all[nlist[0, t, n]])
            xx[0:nrhs, n * tile:(n + 1) * tile] = high
            xx[nrhs:2 * nrhs, n * tile:(n + 1) * tile] = low
        weights = xx[:, :nnb * tile]
        term = fold(nt(fhi[t], weights) + nt(flo[t], weights))
        res_out[0, t] = rhs_all[tlist[0, t]] - term

    rhs_line(False)

    @pl.loop(0, owners)
    def _(c):
        @pl.when(c != q)
        def _():
            rs_copy(c).wait_send()

    df_all(False)
    rhs_plane(False)
    for k in range(rows):
        @pl.when(p == k)
        def _():
            line_send(k, False)
            if k > 0:
                @pl.when(q == k - 1)
                def _():
                    scatter(k, False)

        plane_send(k, False)

    @pl.when(q < p - 1)
    def _():
        v_copy(q).wait_send()


def per_device(rows, cols, window_rhs, past_solution, past_panel, window_panel, diag_inverse, tile_list, neighbor_list, force_constants):
    nrhs, order = window_rhs.shape
    depth = past_solution.shape[1]
    tpd, nnb, tile = force_constants.shape[1:4]
    owners = order // tile
    tiles = rows * owners
    wide = max(order, nnb * tile)
    hbm = pl.BlockSpec(memory_space=pl.ANY)
    smem = pl.BlockSpec(memory_space=pltpu.SMEM)
    vmem = pl.BlockSpec(memory_space=pltpu.VMEM)
    dma = pltpu.SemaphoreType.DMA
    return pl.pallas_call(
        functools.partial(kernel, rows, cols, owners, tile, nrhs, tpd, nnb),
        out_shape=(
            jax.ShapeDtypeStruct((nrhs, order), F32),
            jax.ShapeDtypeStruct((1, tpd, nrhs, tile), F32),
        ),
        in_specs=[hbm, hbm, hbm, hbm, hbm, smem, smem, hbm],
        out_specs=(vmem, vmem),
        scratch_shapes=[
            pltpu.VMEM((nrhs, depth), F32),
            pltpu.VMEM((order, depth), F32),
            pltpu.VMEM((order, order), F32),
            pltpu.VMEM((order, order), F32),
            pltpu.VMEM((tpd, nnb, tile, tile), F32),
            pltpu.VMEM((2 * nrhs, depth), BF16),
            pltpu.VMEM((2 * nrhs, wide), BF16),
            pltpu.VMEM((order, order), BF16),
            pltpu.VMEM((order, order), BF16),
            pltpu.VMEM((order, order), BF16),
            pltpu.VMEM((order, order), BF16),
            pltpu.VMEM((tpd, tile, nnb * tile), BF16),
            pltpu.VMEM((tpd, tile, nnb * tile), BF16),
            pltpu.VMEM((owners, nrhs, tile), F32),
            pltpu.VMEM((cols, nrhs, tile), F32),
            pltpu.VMEM((owners, nrhs, tile), F32),
            pltpu.VMEM((owners, nrhs, tile), F32),
            pltpu.VMEM((owners, nrhs, tile), F32),
            pltpu.VMEM((max(rows - 2, 1), owners, nrhs, tile), F32),
            pltpu.VMEM((tiles, nrhs, tile), F32),
            pltpu.VMEM((tiles, nrhs, tile), F32),
            dma((4,)),
            dma((owners,)),
            dma((owners,)),
            dma((owners,)),
            dma((cols,)),
            dma((cols,)),
            dma((owners,)),
            dma((owners,)),
            dma((rows,)),
            dma((rows, cols)),
            dma((tiles,)),
            dma((rows,)),
            dma((rows, cols)),
            dma((tiles,)),
            dma,
            dma((rows,)),
        ],
        compiler_params=pltpu.CompilerParams(
            collective_id=0, has_side_effects=True, vmem_limit_bytes=52 * 2**20
        ),
    )(window_rhs, past_solution, past_panel, window_panel, diag_inverse, tile_list, neighbor_list, force_constants)


def solution(mesh):
    placed = (
        P(None, "prow"),
        P(None, "pcol"),
        P("prow", "pcol"),
        P("prow", None, "pcol", None),
        P("prow", None, None),
        P(("prow", "pcol"), None),
        P(("prow", "pcol"), None, None),
        P(("prow", "pcol"), None, None, None, None),
    )
    return jax.shard_map(
        functools.partial(per_device, mesh.shape["prow"], mesh.shape["pcol"]),
        mesh=mesh,
        in_specs=placed,
        out_specs=(P(None, "prow"), P(("prow", "pcol"), None, None, None)),
        check_vma=False,
    )
```

time: 454 us -> 73.9 us (0.16)
  waiting for transfers between devices: 402 us -> 0 us
  Pallas kernels: 0 us -> 68.4 us
  matrix products: 21.6 us -> 0 us
  between operations: 14.1 us -> 0.65 us
  local copies, waits for them, and re-layouts: 12.6 us -> 4.65 us
    psum x8 -> x0, waiting for transfers between devices: 375 us -> none  [the longest x4 229 us: per_device(): total = lax.psum(partial_value, 'pcol')]
    pallas_call x0 -> x1, Pallas kernels: none -> 68.4 us  [per_device(): pl.pallas_call(functools.partial(kernel, rows, cols, owners, tile, nrhs,...]
    all_gather x1 -> x0, waiting for transfers between devices: 26.1 us -> none  [per_device(): full_rhs = lax.all_gather(window_rhs, 'prow', axis=1, tiled=True)]
    dot_general x3 -> x0, matrix products: 21.6 us -> none  [the longest x2 18.7 us: right_product(): lax.dot_general(left, right, (((1,), (1,)), ((), ())), precision=lax.Prec...]
  transfers between devices with their start and end apart: 9 -> 0, of which waited for: 9 -> 0; matrix products, arithmetic and copies ran while one was open for 2% -> 0% of each run, Pallas kernels for 0% -> 0%
where the time goes in v1:
time: 73.9 us; the launch traced here: 73.7 us
  Pallas kernels  68.4 us (93%)
  local copies, waits for them, and re-layouts  4.65 us (6%)
    pallas_call x1, Pallas kernels, per_device(): pl.pallas_call(functools.partial(kernel, rows, cols, owners, tile, nrhs,...  68.4 us
    unnamed x10, local copies, waits for them, and re-layouts  4.65 us

profile of v1, /device:TPU:0, one launch (start us, length us, event | category | flops | bytes accessed | tf_op | source)
XLA Modules:
  0.0 73.7 jit_solution(266394017940585724)
XLA Ops:
  0.6 0.0 copy-start
  0.6 1.0 %copy-done = f32[64,2048]{1,0:T(8,128)S(1)} copy-done((f32[64,2048]{1,0:T(8,128)S(1)}, f32[64,2048]{1,0:T(8,128)}, u32[]{:S(2)}) %copy-start) | copy-done | bytes 524312
  1.7 0.0 copy-start.1
  1.7 0.9 %copy-done.1 = f32[64,1024]{1,0:T(8,128)S(1)} copy-done((f32[64,1024]{1,0:T(8,128)S(1)}, f32[64,1024]{1,0:T(8,128)}, u32[]{:S(2)}) %copy-start.1) | copy-done | bytes 262168
  2.6 0.0 copy-start.2
  2.6 0.7 copy-done.2
  3.3 0.0 copy-start.3
  3.3 0.7 copy-done.3
  4.0 68.4 %shard_map.95 = (f32[64,1024]{1,0:T(8,128)S(1)}, f32[1,2,64,128]{3,2,1,0:T(8,128)S(1)}) custom-call(f32[64,1024]{1,0:T(8,128)S(1)} %copy-done.1, f32[64,2048]{1,0:T(8,128)S(1)} %copy-done, f32[1024,2048]{1,0:T(8,128)} %panel_hbm.1, f32[1,1024,1,1024]{3,2,1,0:T(1,128)} %win_hbm.1, f32[1,1024,1024]{2,1,0:T(8,128)} %dinv_hbm.1, s32[1,2]{1,0:T(1,128)S(1)} %copy-done.3, ...), custom_call_target="tpu_custom_call" | custom-call | tf_op jit(solution)/shard_map/pallas_call | solution.py:403
  72.3 0.7 copy.12
  73.0 0.6 copy.13
Async XLA Ops:
  0.6 1.0 %copy-start = (f32[64,2048]{1,0:T(8,128)S(1)}, f32[64,2048]{1,0:T(8,128)}, u32[]{:S(2)}) copy-start(f32[64,2048]{1,0:T(8,128)} %psol_hbm.1) | copy-start | bytes 1572868
  1.7 0.9 %copy-start.1 = (f32[64,1024]{1,0:T(8,128)S(1)}, f32[64,1024]{1,0:T(8,128)}, u32[]{:S(2)}) copy-start(f32[64,1024]{1,0:T(8,128)} %rhs_hbm.1) | copy-start | bytes 786436
  2.6 0.7 copy-start.2
  3.3 0.7 copy-start.3

commit v2 on v1

v2 whole, which is shorter than its diff:
```python
import functools

import jax
import jax.numpy as jnp
from jax import lax
from jax.experimental import pallas as pl
from jax.experimental.pallas import tpu as pltpu
from jax.sharding import PartitionSpec as P

MESH = pl.DeviceIdType.MESH
BF16 = jnp.bfloat16
F32 = jnp.float32


def halves(value):
    high = value.astype(BF16)
    return high, (value - high.astype(F32)).astype(BF16)


def nt(left, right):
    return lax.dot_general(left, right, (((1,), (1,)), ((), ())), preferred_element_type=F32)


def nn(left, right):
    return lax.dot_general(left, right, (((1,), (0,)), ((), ())), preferred_element_type=F32)


def kernel(
    rows, cols, owners, tile, nrhs, tpd, nnb,
    rhs_hbm, psol_hbm, panel_hbm, win_hbm, dinv_hbm, tlist_hbm, nlist_hbm, force_hbm,
    sol_out, res_out,
    tlist, nlist, psol, panel, win, dinv, force, xpast, xx, whi, wlo, mhi, mlo, fhi, flo,
    part, rs_buf, outp, usend, ubuf, vout, vbuf, y_all, rhs_all,
    load_sem, panel_sem, rhs_sem,
    rs_send, rs_recv, df_send, df_recv, dx_send, ch_send, sc_send, ln_send, ag_send, y_recv,
    rl_send, ra_send, r_recv, v_send, v_recv,
):
    p = lax.axis_index("prow")
    q = lax.axis_index("pcol")
    order = owners * tile
    owner = q < owners
    mine = lax.rem(q, owners)
    barrier = pltpu.get_barrier_semaphore()

    def at_plane(step):
        return lax.rem(q + 1 + step, cols)

    def at_line(step):
        return lax.rem(p + 1 + step, rows)

    def remote(src, dst, send, recv, row, col):
        return pltpu.make_async_remote_copy(
            src_ref=src, dst_ref=dst, send_sem=send, recv_sem=recv,
            device_id=(row, col), device_id_type=MESH,
        )

    def act(copy, go):
        if go:
            copy.start()
        else:
            copy.wait_send()

    first = pltpu.make_async_copy(psol_hbm, psol, load_sem.at[0])
    first.start()

    def panel_copy(c):
        at = pl.ds(pl.multiple_of(c * tile, tile), tile)
        return pltpu.make_async_copy(panel_hbm.at[at, :], panel.at[at, :], panel_sem.at[c])

    @pl.loop(0, owners)
    def _(i):
        panel_copy(i).start()

    def rhs_copy(c):
        return pltpu.make_async_copy(
            rhs_hbm.at[:, c * tile:(c + 1) * tile], rhs_all.at[p * owners + c], rhs_sem.at[c]
        )

    for c in range(owners):
        rhs_copy(c).start()
    load_dinv = pltpu.make_async_copy(dinv_hbm.at[0], dinv, load_sem.at[1])
    load_win = pltpu.make_async_copy(win_hbm.at[0, :, 0, :], win, load_sem.at[2])
    load_force = pltpu.make_async_copy(force_hbm.at[0], force, load_sem.at[3])
    load_tlist = pltpu.make_async_copy(tlist_hbm, tlist, load_sem.at[4])
    load_nlist = pltpu.make_async_copy(nlist_hbm, nlist, load_sem.at[5])
    load_dinv.start()
    load_tlist.start()
    load_nlist.start()

    @pl.loop(0, cols - 1)
    def _(i):
        pl.semaphore_signal(barrier, inc=1, device_id=(p, at_plane(i)), device_id_type=MESH)

    @pl.loop(0, rows - 1)
    def _(i):
        pl.semaphore_signal(barrier, inc=1, device_id=(at_line(i), q), device_id_type=MESH)

    @pl.when((p >= 2) & (q == p - 1))
    def _():
        pl.semaphore_signal(barrier, inc=1, device_id=(p - 1, q - 1), device_id_type=MESH)

    @pl.when((p == 1) & (q == 0))
    def _():
        @pl.loop(1, owners)
        def _(c):
            pl.semaphore_signal(barrier, inc=1, device_id=(0, c), device_id_type=MESH)

    first.wait()
    high, low = halves(psol[...])
    xpast[0:nrhs, :] = high
    xpast[nrhs:2 * nrhs, :] = low
    for c in range(owners):
        rhs_copy(c).wait()
    passes_on = ((p == 0) & owner & (q > 0)) | ((p > 0) & (p < rows - 1) & (q == p - 1))
    pl.semaphore_wait(barrier, cols - 1 + rows - 1 + jnp.where(passes_on, 1, 0))

    def rhs_line(go):
        t = p * owners + mine

        @pl.when(owner)
        def _():
            @pl.loop(0, rows - 1)
            def _(i):
                act(remote(rhs_all.at[t], rhs_all.at[t], rl_send.at[i], r_recv.at[t], at_line(i), q), go)

    rhs_line(True)

    def fold(value):
        turned = value.T
        return turned[:nrhs] + turned[nrhs:]

    def pack(ref, base):
        for c in range(owners):
            high, low = halves(ref[base + c])
            xx[0:nrhs, c * tile:(c + 1) * tile] = high
            xx[nrhs:2 * nrhs, c * tile:(c + 1) * tile] = low

    def rs_copy(c):
        return remote(outp.at[c], rs_buf.at[q], rs_send.at[c], rs_recv.at[q], p, c)

    step = min(256, order)
    pair = step // tile

    @pl.loop(0, order // step)
    def _(i):
        for n in range(pair):
            panel_copy(i * pair + n).wait()
        high, low = halves(panel[pl.ds(pl.multiple_of(i * step, step), step), :])
        weights = xpast[...]
        value = nt(high, weights) + nt(low, weights)
        for n in range(pair):
            part[i * pair + n] = fold(value[n * tile:(n + 1) * tile])

    load_win.start()
    load_force.start()

    @pl.when(q == 0)
    def _():
        for c in range(owners):
            part[c] = part[c] - rhs_all[p * owners + c]

    load_dinv.wait()
    pack(part, 0)
    for at in range(0, order, step):
        depth = at + step
        high, low = halves(dinv[at:depth, :depth])
        weights = xx[:, :depth]
        value = nt(high, weights) + nt(low, weights)
        for n in range(pair):
            c = at // tile + n
            outp[c] = fold(value[n * tile:(n + 1) * tile])

            @pl.when(c != q)
            def _():
                rs_copy(c).start()

    load_win.wait()

    @pl.when(q < p)
    def _():
        for at in range(0, order, step):
            high, low = halves(win[at:at + step, :])
            whi[at:at + step, :] = high
            wlo[at:at + step, :] = low
        for at in range(0, order, step):
            depth = at + step
            high, low = halves(dinv[at:at + step, :depth])
            value = nn(high, whi[:depth, :]) + nn(low, whi[:depth, :]) + nn(high, wlo[:depth, :])
            high, low = halves(value)
            mhi[at:at + step, :] = high
            mlo[at:at + step, :] = low

    solver = (p > 0) & (q == p - 1)

    def df_send_one(go):
        @pl.when(owner & (p > 0) & jnp.logical_not(solver))
        def _():
            act(remote(usend, ubuf.at[mine], df_send, df_recv.at[mine], p, p - 1), go)

    def first_send(go):
        @pl.when(owner & (p == 0))
        def _():
            act(remote(y_all.at[mine], y_all.at[mine], dx_send.at[mine], y_recv.at[mine], 1, 0), go)

    def line_send(k, go):
        t = k * owners + mine

        @pl.when(owner)
        def _():
            @pl.loop(0, rows - 1)
            def _(i):
                @pl.when((q != k) | (at_line(i) < k))
                def _():
                    act(remote(y_all.at[t], y_all.at[t], ln_send.at[i], y_recv.at[t], at_line(i), q), go)

    def has_whole(k, row, col):
        handed = (row > k) & (col == k)
        return handed if k == 0 else handed | ((row == k) & (col == k - 1))

    def plane_send(k, go):
        t = k * owners + mine

        @pl.when(owner)
        def _():
            @pl.loop(0, cols - 1)
            def _(i):
                d = at_plane(i)

                @pl.when(jnp.logical_not(has_whole(k, p, d)))
                def _():
                    act(remote(y_all.at[t], y_all.at[t], ag_send.at[k, i], y_recv.at[t], p, d), go)

    def solved_send(k, c, go):
        t = k * owners + c
        if k < rows - 1:
            act(remote(y_all.at[t], y_all.at[t], dx_send.at[c], y_recv.at[t], p + 1, k), go)

        @pl.when(c != q)
        def _():
            act(remote(y_all.at[t], y_all.at[t], sc_send.at[c], y_recv.at[t], p, c), go)

    def chain_send(k, c, go):
        t = k * owners + c

        @pl.when(p < rows - 1)
        def _():
            act(remote(y_all.at[t], y_all.at[t], ch_send.at[c], y_recv.at[t], p + 1, q), go)

    def v_send_one(j, c, go):
        act(remote(vout.at[c], vbuf.at[j, c], v_send.at[c], v_recv.at[j, c], p, p - 1), go)

    def y_wait(t):
        remote(y_all.at[t], y_all.at[t], ln_send.at[0], y_recv.at[t], p, at_plane(0)).wait_recv()

    def rhs_plane(go):
        @pl.when(owner)
        def _():
            @pl.loop(0, rows - 1)
            def _(j):
                t = at_line(j) * owners + mine
                if go:
                    remote(rhs_all.at[t], rhs_all.at[t], rl_send.at[0], r_recv.at[t], p, at_plane(0)).wait_recv()

                @pl.loop(0, cols - 1)
                def _(i):
                    act(remote(rhs_all.at[t], rhs_all.at[t], ra_send.at[j, i], r_recv.at[t], p, at_plane(i)), go)

    @pl.when(owner)
    def _():
        @pl.loop(0, cols - 1)
        def _(i):
            s = at_plane(i)
            remote(outp.at[mine], rs_buf.at[s], rs_send.at[mine], rs_recv.at[s], p, s).wait_recv()

        total = outp[mine]
        for i in range(cols - 1):
            total = total + rs_buf[at_plane(i)]

        @pl.when(p == 0)
        def _():
            y_all[mine] = -total

        @pl.when(solver)
        def _():
            ubuf[mine] = -total

        @pl.when((p > 0) & jnp.logical_not(solver))
        def _():
            usend[...] = -total

    first_send(True)
    df_send_one(True)

    @pl.when(p >= 2)
    def _():
        rhs_plane(True)

    @pl.when(solver)
    def _():
        for c in range(owners):
            @pl.when(c != q)
            def _():
                remote(usend, ubuf.at[c], df_send, df_recv.at[c], p, at_plane(0)).wait_recv()

    for k in range(rows):
        base = k * owners
        handed = (p > k) & (q == k)
        made = p == k if k == 0 else (p == k) & (q == k - 1)

        @pl.when(handed)
        def _():
            @pl.loop(0, owners)
            def _(c):
                y_wait(base + c)
                chain_send(k, c, True)

            pack(y_all, base)
            weights = xx[...]

            def product(c):
                at = pl.ds(pl.multiple_of(c * tile, tile), tile)
                return fold(nt(mhi[at, :], weights) + nt(mlo[at, :], weights))

            @pl.when(p == k + 1)
            def _():
                for j in range(k):
                    @pl.loop(0, owners)
                    def _(c):
                        remote(vout.at[c], vbuf.at[j, c], v_send.at[c], v_recv.at[j, c], p, at_plane(0)).wait_recv()

                @pl.loop(0, owners)
                def _(c):
                    value = ubuf[c] - product(c)
                    for j in range(k):
                        value = value - vbuf[j, c]
                    y_all[base + owners + c] = value
                    if k < rows - 1:
                        solved_send(k + 1, c, True)

            @pl.when(p > k + 1)
            def _():
                @pl.loop(0, owners)
                def _(c):
                    vout[c] = product(c)
                    v_send_one(k, c, True)

        @pl.when(owner & jnp.logical_not(made | handed))
        def _():
            y_wait(base + mine)

        @pl.when(p == k)
        def _():
            line_send(k, True)

        plane_send(k, True)

        @pl.when((p == k) & (p < 2))
        def _():
            rhs_plane(True)

    load_force.wait()
    for t in range(tpd):
        for n in range(nnb):
            high, low = halves(force[t, n])
            fhi[t, :, n * tile:(n + 1) * tile] = high
            flo[t, :, n * tile:(n + 1) * tile] = low

    for k in range(rows):
        @pl.when(jnp.logical_not(has_whole(k, p, q)))
        def _():
            @pl.loop(0, cols - 1)
            def _(i):
                c = at_plane(i)

                @pl.when(c < owners)
                def _():
                    y_wait(k * owners + c)

    for c in range(owners):
        sol_out[:, c * tile:(c + 1) * tile] = y_all[p * owners + c]

    load_tlist.wait()
    load_nlist.wait()

    @pl.loop(0, rows - 1)
    def _(j):
        @pl.loop(0, cols - 1)
        def _(i):
            c = at_plane(i)

            @pl.when(c < owners)
            def _():
                t = at_line(j) * owners + c
                remote(rhs_all.at[t], rhs_all.at[t], rl_send.at[0], r_recv.at[t], p, at_plane(0)).wait_recv()

    for t in range(tpd):
        for n in range(nnb):
            high, low = halves(y_all[nlist[0, t, n]])
            xx[0:nrhs, n * tile:(n + 1) * tile] = high
            xx[nrhs:2 * nrhs, n * tile:(n + 1) * tile] = low
        weights = xx[:, :nnb * tile]
        term = fold(nt(fhi[t], weights) + nt(flo[t], weights))
        res_out[0, t] = rhs_all[tlist[0, t]] - term

    rhs_line(False)

    @pl.loop(0, owners)
    def _(c):
        @pl.when(c != q)
        def _():
            rs_copy(c).wait_send()

    first_send(False)
    df_send_one(False)
    rhs_plane(False)
    for k in range(rows):
        @pl.when(p == k)
        def _():
            line_send(k, False)

        if k > 0:
            @pl.when((p == k) & (q == k - 1))
            def _():
                @pl.loop(0, owners)
                def _(c):
                    solved_send(k, c, False)

        @pl.when((p > k) & (q == k))
        def _():
            @pl.loop(0, owners)
            def _(c):
                chain_send(k, c, False)

                @pl.when(p > k + 1)
                def _():
                    v_send_one(k, c, False)

        plane_send(k, False)


def per_device(rows, cols, window_rhs, past_solution, past_panel, window_panel, diag_inverse, tile_list, neighbor_list, force_constants):
    nrhs, order = window_rhs.shape
    depth = past_solution.shape[1]
    tpd, nnb, tile = force_constants.shape[1:4]
    owners = order // tile
    tiles = rows * owners
    wide = max(order, nnb * tile)
    hbm = pl.BlockSpec(memory_space=pltpu.HBM)
    vmem = pl.BlockSpec(memory_space=pltpu.VMEM)
    dma = pltpu.SemaphoreType.DMA
    return pl.pallas_call(
        functools.partial(kernel, rows, cols, owners, tile, nrhs, tpd, nnb),
        out_shape=(
            jax.ShapeDtypeStruct((nrhs, order), F32),
            jax.ShapeDtypeStruct((1, tpd, nrhs, tile), F32),
        ),
        in_specs=[hbm] * 8,
        out_specs=(vmem, vmem),
        scratch_shapes=[
            pltpu.SMEM((1, tpd), jnp.int32),
            pltpu.SMEM((1, tpd, nnb), jnp.int32),
            pltpu.VMEM((nrhs, depth), F32),
            pltpu.VMEM((order, depth), F32),
            pltpu.VMEM((order, order), F32),
            pltpu.VMEM((order, order), F32),
            pltpu.VMEM((tpd, nnb, tile, tile), F32),
            pltpu.VMEM((2 * nrhs, depth), BF16),
            pltpu.VMEM((2 * nrhs, wide), BF16),
            pltpu.VMEM((order, order), BF16),
            pltpu.VMEM((order, order), BF16),
            pltpu.VMEM((order, order), BF16),
            pltpu.VMEM((order, order), BF16),
            pltpu.VMEM((tpd, tile, nnb * tile), BF16),
            pltpu.VMEM((tpd, tile, nnb * tile), BF16),
            pltpu.VMEM((owners, nrhs, tile), F32),
            pltpu.VMEM((cols, nrhs, tile), F32),
            pltpu.VMEM((owners, nrhs, tile), F32),
            pltpu.VMEM((nrhs, tile), F32),
            pltpu.VMEM((owners, nrhs, tile), F32),
            pltpu.VMEM((owners, nrhs, tile), F32),
            pltpu.VMEM((max(rows - 2, 1), owners, nrhs, tile), F32),
            pltpu.VMEM((tiles, nrhs, tile), F32),
            pltpu.VMEM((tiles, nrhs, tile), F32),
            dma((6,)),
            dma((owners,)),
            dma((owners,)),
            dma((owners,)),
            dma((cols,)),
            dma,
            dma((owners,)),
            dma((owners,)),
            dma((owners,)),
            dma((owners,)),
            dma((rows,)),
            dma((rows, cols)),
            dma((tiles,)),
            dma((rows,)),
            dma((rows, cols)),
            dma((tiles,)),
            dma((owners,)),
            dma((rows, owners)),
        ],
        compiler_params=pltpu.CompilerParams(
            collective_id=0, has_side_effects=True, vmem_limit_bytes=63 * 2**20
        ),
    )(window_rhs, past_solution, past_panel, window_panel, diag_inverse, tile_list, neighbor_list, force_constants)


def solution(mesh):
    placed = (
        P(None, "prow"),
        P(None, "pcol"),
        P("prow", "pcol"),
        P("prow", None, "pcol", None),
        P("prow", None, None),
        P(("prow", "pcol"), None),
        P(("prow", "pcol"), None, None),
        P(("prow", "pcol"), None, None, None, None),
    )
    return jax.shard_map(
        functools.partial(per_device, mesh.shape["prow"], mesh.shape["pcol"]),
        mesh=mesh,
        in_specs=placed,
        out_specs=(P(None, "prow"), P(("prow", "pcol"), None, None, None)),
        check_vma=False,
    )
```

time: 73.9 us -> 64.5 us (0.87)
  Pallas kernels: 68.4 us -> 60.5 us
  local copies, waits for them, and re-layouts: 4.65 us -> 3.14 us
    pallas_call x1, Pallas kernels: 68.4 us -> 60.5 us  [per_device(): pl.pallas_call(functools.partial(kernel, rows, cols, owners, tile, nrhs,...]
    unnamed x10 -> x2, local copies, waits for them, and re-layouts: 4.65 us -> 3.14 us
where the time goes in v2:
time: 64.5 us; the launch traced here: 64.3 us
  Pallas kernels  60.5 us (94%)
  local copies, waits for them, and re-layouts  3.14 us (5%)
    pallas_call x1, Pallas kernels, per_device(): pl.pallas_call(functools.partial(kernel, rows, cols, owners, tile, nrhs,...  60.5 us
    unnamed x2, local copies, waits for them, and re-layouts  3.14 us

profile of v2, /device:TPU:0, one launch (start us, length us, event | category | flops | bytes accessed | tf_op | source)
XLA Modules:
  0.0 64.3 jit_solution(14204426696727317318)
XLA Ops:
  0.6 60.5 %shard_map.95 = (f32[64,1024]{1,0:T(8,128)}, f32[1,2,64,128]{3,2,1,0:T(8,128)}) custom-call(f32[64,1024]{1,0:T(8,128)} %rhs_hbm.1, f32[64,2048]{1,0:T(8,128)} %psol_hbm.1, f32[1024,2048]{1,0:T(8,128)} %panel_hbm.1, f32[1,1024,1,1024]{3,2,1,0:T(1,128)} %win_hbm.1, f32[1,1024,1024]{2,1,0:T(8,128)} %dinv_hbm.1, s32[1,2]{1,0:T(1,128)} %tlist_hbm.1, ...), custom_call_target="tpu_custom_call" | custom-call | tf_op jit(solution)/shard_map/pallas_call | solution.py:451
  61.1 1.7 %copy.12 = f32[64,1024]{1,0:T(8,128)} copy(f32[64,1024]{1,0:T(8,128)} %get-tuple-element.4) | data formatting | bytes 524288
  62.8 1.5 %copy.13 = f32[1,2,64,128]{3,2,1,0:T(8,128)} copy(f32[1,2,64,128]{3,2,1,0:T(8,128)} %get-tuple-element.5) | data formatting | bytes 131072

commit v3 on v2

--- a/solution.py
+++ b/solution.py
@@ -17,12 +17,13 @@
     return high, (value - high.astype(F32)).astype(BF16)
 
 
-def nt(left, right):
-    return lax.dot_general(left, right, (((1,), (1,)), ((), ())), preferred_element_type=F32)
-
-
 def nn(left, right):
     return lax.dot_general(left, right, (((1,), (0,)), ((), ())), preferred_element_type=F32)
+
+
+def turned(block):
+    high = block.astype(BF16).astype(F32)
+    return jnp.concatenate([high, block - high], axis=0).T.astype(BF16)
 
 
 def kernel(
@@ -83,6 +84,10 @@
     load_force = pltpu.make_async_copy(force_hbm.at[0], force, load_sem.at[3])
     load_tlist = pltpu.make_async_copy(tlist_hbm, tlist, load_sem.at[4])
     load_nlist = pltpu.make_async_copy(nlist_hbm, nlist, load_sem.at[5])
+    @pl.when(q < p)
+    def _():
+        load_win.start()
+
     load_dinv.start()
     load_tlist.start()
     load_nlist.start()
@@ -106,9 +111,8 @@
             pl.semaphore_signal(barrier, inc=1, device_id=(0, c), device_id_type=MESH)
 
     first.wait()
-    high, low = halves(psol[...])
-    xpast[0:nrhs, :] = high
-    xpast[nrhs:2 * nrhs, :] = low
+    for at in range(0, psol.shape[1], tile):
+        xpast[at:at + tile, :] = turned(psol[:, at:at + tile])
     for c in range(owners):
         rhs_copy(c).wait()
     passes_on = ((p == 0) & owner & (q > 0)) | ((p > 0) & (p < rows - 1) & (q == p - 1))
@@ -131,9 +135,7 @@
 
     def pack(ref, base):
         for c in range(owners):
-            high, low = halves(ref[base + c])
-            xx[0:nrhs, c * tile:(c + 1) * tile] = high
-            xx[nrhs:2 * nrhs, c * tile:(c + 1) * tile] = low
+            xx[c * tile:(c + 1) * tile, :] = turned(ref[base + c])
 
     def rs_copy(c):
         return remote(outp.at[c], rs_buf.at[q], rs_send.at[c], rs_recv.at[q], p, c)
@@ -147,11 +149,10 @@
             panel_copy(i * pair + n).wait()
         high, low = halves(panel[pl.ds(pl.multiple_of(i * step, step), step), :])
         weights = xpast[...]
-        value = nt(high, weights) + nt(low, weights)
+        value = nn(high, weights) + nn(low, weights)
         for n in range(pair):
             part[i * pair + n] = fold(value[n * tile:(n + 1) * tile])
 
-    load_win.start()
     load_force.start()
 
     @pl.when(q == 0)
@@ -164,8 +165,8 @@
     for at in range(0, order, step):
         depth = at + step
         high, low = halves(dinv[at:depth, :depth])
-        weights = xx[:, :depth]
-        value = nt(high, weights) + nt(low, weights)
+        weights = xx[:depth, :]
+        value = nn(high, weights) + nn(low, weights)
         for n in range(pair):
             c = at // tile + n
             outp[c] = fold(value[n * tile:(n + 1) * tile])
@@ -174,10 +175,9 @@
             def _():
                 rs_copy(c).start()
 
-    load_win.wait()
-
     @pl.when(q < p)
     def _():
+        load_win.wait()
         for at in range(0, order, step):
             high, low = halves(win[at:at + step, :])
             whi[at:at + step, :] = high
@@ -309,17 +309,14 @@
 
         @pl.when(handed)
         def _():
-            @pl.loop(0, owners)
-            def _(c):
+            for c in range(owners):
                 y_wait(base + c)
                 chain_send(k, c, True)
-
-            pack(y_all, base)
-            weights = xx[...]
-
-            def product(c):
-                at = pl.ds(pl.multiple_of(c * tile, tile), tile)
-                return fold(nt(mhi[at, :], weights) + nt(mlo[at, :], weights))
+                xx[c * tile:(c + 1) * tile, :] = turned(y_all[base + c])
+
+            def product(at):
+                weights = xx[:order, :]
+                return nn(mhi[at:at + step, :], weights) + nn(mlo[at:at + step, :], weights)
 
             @pl.when(p == k + 1)
             def _():
@@ -328,21 +325,25 @@
                     def _(c):
                         remote(vout.at[c], vbuf.at[j, c], v_send.at[c], v_recv.at[j, c], p, at_plane(0)).wait_recv()
 
-                @pl.loop(0, owners)
-                def _(c):
-                    value = ubuf[c] - product(c)
-                    for j in range(k):
-                        value = value - vbuf[j, c]
-                    y_all[base + owners + c] = value
-                    if k < rows - 1:
-                        solved_send(k + 1, c, True)
+                for at in range(0, order, step):
+                    whole = product(at)
+                    for n in range(pair):
+                        c = at // tile + n
+                        value = ubuf[c] - fold(whole[n * tile:(n + 1) * tile])
+                        for j in range(k):
+                            value = value - vbuf[j, c]
+                        y_all[base + owners + c] = value
+                        if k < rows - 1:
+                            solved_send(k + 1, c, True)
 
             @pl.when(p > k + 1)
             def _():
-                @pl.loop(0, owners)
-                def _(c):
-                    vout[c] = product(c)
-                    v_send_one(k, c, True)
+                for at in range(0, order, step):
+                    whole = product(at)
+                    for n in range(pair):
+                        c = at // tile + n
+                        vout[c] = fold(whole[n * tile:(n + 1) * tile])
+                        v_send_one(k, c, True)
 
         @pl.when(owner & jnp.logical_not(made | handed))
         def _():
@@ -394,12 +395,8 @@
                 remote(rhs_all.at[t], rhs_all.at[t], rl_send.at[0], r_recv.at[t], p, at_plane(0)).wait_recv()
 
     for t in range(tpd):
-        for n in range(nnb):
-            high, low = halves(y_all[nlist[0, t, n]])
-            xx[0:nrhs, n * tile:(n + 1) * tile] = high
-            xx[nrhs:2 * nrhs, n * tile:(n + 1) * tile] = low
-        weights = xx[:, :nnb * tile]
-        term = fold(nt(fhi[t], weights) + nt(flo[t], weights))
+        weights = jnp.concatenate([turned(y_all[nlist[0, t, n]]) for n in range(nnb)], axis=0)
+        term = fold(nn(fhi[t], weights) + nn(flo[t], weights))
         res_out[0, t] = rhs_all[tlist[0, t]] - term
 
     rhs_line(False)
@@ -444,7 +441,6 @@
     tpd, nnb, tile = force_constants.shape[1:4]
     owners = order // tile
     tiles = rows * owners
-    wide = max(order, nnb * tile)
     hbm = pl.BlockSpec(memory_space=pltpu.HBM)
     vmem = pl.BlockSpec(memory_space=pltpu.VMEM)
     dma = pltpu.SemaphoreType.DMA
@@ -464,8 +460,8 @@
             pltpu.VMEM((order, order), F32),
             pltpu.VMEM((order, order), F32),
             pltpu.VMEM((tpd, nnb, tile, tile), F32),
-            pltpu.VMEM((2 * nrhs, depth), BF16),
-            pltpu.VMEM((2 * nrhs, wide), BF16),
+            pltpu.VMEM((depth, 2 * nrhs), BF16),
+            pltpu.VMEM((order, 2 * nrhs), BF16),
             pltpu.VMEM((order, order), BF16),
             pltpu.VMEM((order, order), BF16),
             pltpu.VMEM((order, order), BF16),

time: 64.5 us -> 63.1 us (0.978)
  Pallas kernels: 60.5 us -> 59 us
    pallas_call x1, Pallas kernels: 60.5 us -> 59 us  [per_device(): pl.pallas_call(functools.partial(kernel, rows, cols, owners, tile, nrhs,...]
where the time goes in v3:
time: 63.1 us; the launch traced here: 62.8 us
  Pallas kernels  59 us (94%)
  local copies, waits for them, and re-layouts  3.14 us (5%)
  between operations  0.64 us (1%)
    pallas_call x1, Pallas kernels, per_device(): pl.pallas_call(functools.partial(kernel, rows, cols, owners, tile, nrhs,...  59 us
    unnamed x2, local copies, waits for them, and re-layouts  3.14 us

profile of v3, /device:TPU:0, one launch (start us, length us, event | category | flops | bytes accessed | tf_op | source)
XLA Modules:
  0.0 62.8 jit_solution(4248550890434878432)
XLA Ops:
  0.6 59.0 %shard_map.95 = (f32[64,1024]{1,0:T(8,128)}, f32[1,2,64,128]{3,2,1,0:T(8,128)}) custom-call(f32[64,1024]{1,0:T(8,128)} %rhs_hbm.1, f32[64,2048]{1,0:T(8,128)} %psol_hbm.1, f32[1024,2048]{1,0:T(8,128)} %panel_hbm.1, f32[1,1024,1,1024]{3,2,1,0:T(1,128)} %win_hbm.1, f32[1,1024,1024]{2,1,0:T(8,128)} %dinv_hbm.1, s32[1,2]{1,0:T(1,128)} %tlist_hbm.1, ...), custom_call_target="tpu_custom_call" | custom-call | tf_op jit(solution)/shard_map/pallas_call | solution.py:447
  59.7 1.7 %copy.12 = f32[64,1024]{1,0:T(8,128)} copy(f32[64,1024]{1,0:T(8,128)} %get-tuple-element.4) | data formatting | bytes 524288
  61.4 1.5 %copy.13 = f32[1,2,64,128]{3,2,1,0:T(8,128)} copy(f32[1,2,64,128]{3,2,1,0:T(8,128)} %get-tuple-element.5) | data formatting | bytes 131072

commit v4 on v3

--- a/solution.py
+++ b/solution.py
@@ -30,7 +30,7 @@
     rows, cols, owners, tile, nrhs, tpd, nnb,
     rhs_hbm, psol_hbm, panel_hbm, win_hbm, dinv_hbm, tlist_hbm, nlist_hbm, force_hbm,
     sol_out, res_out,
-    tlist, nlist, psol, panel, win, dinv, force, xpast, xx, whi, wlo, mhi, mlo, fhi, flo,
+    tlist, nlist, psol, panel, win, dinv, force, xpast, xx, whi, wlo, mhi, mlo, fhi, flo, acc,
     part, rs_buf, outp, usend, ubuf, vout, vbuf, y_all, rhs_all,
     load_sem, panel_sem, rhs_sem,
     rs_send, rs_recv, df_send, df_recv, dx_send, ch_send, sc_send, ln_send, ag_send, y_recv,
@@ -84,11 +84,11 @@
     load_force = pltpu.make_async_copy(force_hbm.at[0], force, load_sem.at[3])
     load_tlist = pltpu.make_async_copy(tlist_hbm, tlist, load_sem.at[4])
     load_nlist = pltpu.make_async_copy(nlist_hbm, nlist, load_sem.at[5])
+
     @pl.when(q < p)
     def _():
         load_win.start()
 
-    load_dinv.start()
     load_tlist.start()
     load_nlist.start()
 
@@ -113,10 +113,6 @@
     first.wait()
     for at in range(0, psol.shape[1], tile):
         xpast[at:at + tile, :] = turned(psol[:, at:at + tile])
-    for c in range(owners):
-        rhs_copy(c).wait()
-    passes_on = ((p == 0) & owner & (q > 0)) | ((p > 0) & (p < rows - 1) & (q == p - 1))
-    pl.semaphore_wait(barrier, cols - 1 + rows - 1 + jnp.where(passes_on, 1, 0))
 
     def rhs_line(go):
         t = p * owners + mine
@@ -126,8 +122,6 @@
             @pl.loop(0, rows - 1)
             def _(i):
                 act(remote(rhs_all.at[t], rhs_all.at[t], rl_send.at[i], r_recv.at[t], at_line(i), q), go)
-
-    rhs_line(True)
 
     def fold(value):
         turned = value.T
@@ -147,6 +141,11 @@
     def _(i):
         for n in range(pair):
             panel_copy(i * pair + n).wait()
+
+        @pl.when(i == max(order // step // 2 - 1, 0))
+        def _():
+            load_dinv.start()
+
         high, low = halves(panel[pl.ds(pl.multiple_of(i * step, step), step), :])
         weights = xpast[...]
         value = nn(high, weights) + nn(low, weights)
@@ -154,6 +153,12 @@
             part[i * pair + n] = fold(value[n * tile:(n + 1) * tile])
 
     load_force.start()
+    for c in range(owners):
+        rhs_copy(c).wait()
+    passes_on = ((p == 0) & owner & (q > 0)) | ((p > 0) & (p < rows - 1) & (q == p - 1))
+    pl.semaphore_wait(barrier, cols - 1 + rows - 1 + jnp.where(passes_on, 1, 0))
+
+    rhs_line(True)
 
     @pl.when(q == 0)
     def _():
@@ -309,14 +314,22 @@
 
         @pl.when(handed)
         def _():
-            for c in range(owners):
-                y_wait(base + c)
-                chain_send(k, c, True)
-                xx[c * tile:(c + 1) * tile, :] = turned(y_all[base + c])
+            last = order - step
+            for at in range(0, order, step):
+                for n in range(pair):
+                    c = at // tile + n
+                    y_wait(base + c)
+                    chain_send(k, c, True)
+                    xx[c * tile:(c + 1) * tile, :] = turned(y_all[base + c])
+                if at < last:
+                    weights = xx[at:at + step, :]
+                    value = nn(mhi[:, at:at + step], weights) + nn(mlo[:, at:at + step], weights)
+                    acc[...] = value if at == 0 else acc[...] + value
 
             def product(at):
-                weights = xx[:order, :]
-                return nn(mhi[at:at + step, :], weights) + nn(mlo[at:at + step, :], weights)
+                weights = xx[last:, :]
+                value = nn(mhi[at:at + step, last:], weights) + nn(mlo[at:at + step, last:], weights)
+                return acc[at:at + step, :] + value
 
             @pl.when(p == k + 1)
             def _():
@@ -468,6 +481,7 @@
             pltpu.VMEM((order, order), BF16),
             pltpu.VMEM((tpd, tile, nnb * tile), BF16),
             pltpu.VMEM((tpd, tile, nnb * tile), BF16),
+            pltpu.VMEM((order, 2 * nrhs), F32),
             pltpu.VMEM((owners, nrhs, tile), F32),
             pltpu.VMEM((cols, nrhs, tile), F32),
             pltpu.VMEM((owners, nrhs, tile), F32),

time: 63.1 us -> 61.8 us (0.979)
  Pallas kernels: 59 us -> 57.8 us
    pallas_call x1, Pallas kernels: 59 us -> 57.8 us  [per_device(): pl.pallas_call(functools.partial(kernel, rows, cols, owners, tile, nrhs,...]
where the time goes in v4:
time: 61.8 us; the launch traced here: 61.6 us
  Pallas kernels  57.8 us (94%)
  local copies, waits for them, and re-layouts  3.14 us (5%)
  between operations  0.64 us (1%)
    pallas_call x1, Pallas kernels, per_device(): pl.pallas_call(functools.partial(kernel, rows, cols, owners, tile, nrhs,...  57.8 us
    unnamed x2, local copies, waits for them, and re-layouts  3.14 us

profile of v4, /device:TPU:0, one launch (start us, length us, event | category | flops | bytes accessed | tf_op | source)
XLA Modules:
  0.0 61.6 jit_solution(3532500055183204823)
XLA Ops:
  0.6 57.8 %shard_map.95 = (f32[64,1024]{1,0:T(8,128)}, f32[1,2,64,128]{3,2,1,0:T(8,128)}) custom-call(f32[64,1024]{1,0:T(8,128)} %rhs_hbm.1, f32[64,2048]{1,0:T(8,128)} %psol_hbm.1, f32[1024,2048]{1,0:T(8,128)} %panel_hbm.1, f32[1,1024,1,1024]{3,2,1,0:T(1,128)} %win_hbm.1, f32[1,1024,1024]{2,1,0:T(8,128)} %dinv_hbm.1, s32[1,2]{1,0:T(1,128)} %tlist_hbm.1, ...), custom_call_target="tpu_custom_call" | custom-call | tf_op jit(solution)/shard_map/pallas_call | solution.py:460
  58.5 1.7 %copy.12 = f32[64,1024]{1,0:T(8,128)} copy(f32[64,1024]{1,0:T(8,128)} %get-tuple-element.4) | data formatting | bytes 524288
  60.1 1.5 %copy.13 = f32[1,2,64,128]{3,2,1,0:T(8,128)} copy(f32[1,2,64,128]{3,2,1,0:T(8,128)} %get-tuple-element.5) | data formatting | bytes 131072

commit v5 on v4

--- a/solution.py
+++ b/solution.py
@@ -180,7 +180,18 @@
             def _():
                 rs_copy(c).start()
 
-    @pl.when(q < p)
+    @pl.when((p == 1) & (q == 0))
+    def _():
+        load_win.wait()
+        for at in range(0, order, step):
+            high, low = halves(win[at:at + step, :])
+            mhi[at:at + step, :] = high
+            mlo[at:at + step, :] = low
+            high, low = halves(dinv[at:at + step, :])
+            whi[at:at + step, :] = high
+            wlo[at:at + step, :] = low
+
+    @pl.when((q < p) & (p > 1))
     def _():
         load_win.wait()
         for at in range(0, order, step):
@@ -338,8 +349,19 @@
                     def _(c):
                         remote(vout.at[c], vbuf.at[j, c], v_send.at[c], v_recv.at[j, c], p, at_plane(0)).wait_recv()
 
+                if k == 0:
+                    for at in range(0, order, step):
+                        whole = product(at)
+                        for n in range(pair):
+                            part[at // tile + n] = fold(whole[n * tile:(n + 1) * tile])
+                    pack(part, 0)
+
                 for at in range(0, order, step):
-                    whole = product(at)
+                    if k == 0:
+                        weights = xx[:at + step, :]
+                        whole = nn(whi[at:at + step, :at + step], weights) + nn(wlo[at:at + step, :at + step], weights)
+                    else:
+                        whole = product(at)
                     for n in range(pair):
                         c = at // tile + n
                         value = ubuf[c] - fold(whole[n * tile:(n + 1) * tile])

time: 61.8 us -> 62 us (level)
  no operation moved by 1% of the time
where the time goes in v5:
time: 62 us; the launch traced here: 61.8 us
  Pallas kernels  58 us (94%)
  local copies, waits for them, and re-layouts  3.14 us (5%)
  between operations  0.64 us (1%)
    pallas_call x1, Pallas kernels, per_device(): pl.pallas_call(functools.partial(kernel, rows, cols, owners, tile, nrhs,...  58 us
    unnamed x2, local copies, waits for them, and re-layouts  3.14 us

profile of v5, /device:TPU:0, one launch (start us, length us, event | category | flops | bytes accessed | tf_op | source)
XLA Modules:
  0.0 61.8 jit_solution(7018034098303047991)
XLA Ops:
  0.6 58.0 %shard_map.95 = (f32[64,1024]{1,0:T(8,128)}, f32[1,2,64,128]{3,2,1,0:T(8,128)}) custom-call(f32[64,1024]{1,0:T(8,128)} %rhs_hbm.1, f32[64,2048]{1,0:T(8,128)} %psol_hbm.1, f32[1024,2048]{1,0:T(8,128)} %panel_hbm.1, f32[1,1024,1,1024]{3,2,1,0:T(1,128)} %win_hbm.1, f32[1,1024,1024]{2,1,0:T(8,128)} %dinv_hbm.1, s32[1,2]{1,0:T(1,128)} %tlist_hbm.1, ...), custom_call_target="tpu_custom_call" | custom-call | tf_op jit(solution)/shard_map/pallas_call | solution.py:482
  58.6 1.7 %copy.12 = f32[64,1024]{1,0:T(8,128)} copy(f32[64,1024]{1,0:T(8,128)} %get-tuple-element.4) | data formatting | bytes 524288
  60.3 1.5 %copy.13 = f32[1,2,64,128]{3,2,1,0:T(8,128)} copy(f32[1,2,64,128]{3,2,1,0:T(8,128)} %get-tuple-element.5) | data formatting | bytes 131072

commit v6 on v4

--- a/solution.py
+++ b/solution.py
@@ -61,6 +61,9 @@
         else:
             copy.wait_send()
 
+    def piece(i, size):
+        return pl.ds(pl.multiple_of(i * size, size), size)
+
     first = pltpu.make_async_copy(psol_hbm, psol, load_sem.at[0])
     first.start()
 
@@ -111,8 +114,11 @@
             pl.semaphore_signal(barrier, inc=1, device_id=(0, c), device_id_type=MESH)
 
     first.wait()
-    for at in range(0, psol.shape[1], tile):
-        xpast[at:at + tile, :] = turned(psol[:, at:at + tile])
+    @pl.loop(0, psol.shape[1] // tile)
+    def _(i):
+        at = piece(i, tile)
+        xpast[at, :] = turned(psol[:, at])
+
 
     def rhs_line(go):
         t = p * owners + mine
@@ -128,8 +134,9 @@
         return turned[:nrhs] + turned[nrhs:]
 
     def pack(ref, base):
-        for c in range(owners):
-            xx[c * tile:(c + 1) * tile, :] = turned(ref[base + c])
+        @pl.loop(0, owners)
+        def _(c):
+            xx[piece(c, tile), :] = turned(ref[base + c])
 
     def rs_copy(c):
         return remote(outp.at[c], rs_buf.at[q], rs_send.at[c], rs_recv.at[q], p, c)
@@ -167,13 +174,18 @@
 
     load_dinv.wait()
     pack(part, 0)
-    for at in range(0, order, step):
-        depth = at + step
-        high, low = halves(dinv[at:depth, :depth])
-        weights = xx[:depth, :]
-        value = nn(high, weights) + nn(low, weights)
+    blocks = order // step
+
+    @pl.loop(0, blocks)
+    def _(i):
+        def add(j, value):
+            high, low = halves(dinv[piece(i, step), piece(j, step)])
+            weights = xx[piece(j, step), :]
+            return value + nn(high, weights) + nn(low, weights)
+
+        value = lax.fori_loop(0, i + 1, add, jnp.zeros((step, 2 * nrhs), F32))
         for n in range(pair):
-            c = at // tile + n
+            c = i * pair + n
             outp[c] = fold(value[n * tile:(n + 1) * tile])
 
             @pl.when(c != q)
@@ -183,17 +195,25 @@
     @pl.when(q < p)
     def _():
         load_win.wait()
-        for at in range(0, order, step):
-            high, low = halves(win[at:at + step, :])
-            whi[at:at + step, :] = high
-            wlo[at:at + step, :] = low
-        for at in range(0, order, step):
-            depth = at + step
-            high, low = halves(dinv[at:at + step, :depth])
-            value = nn(high, whi[:depth, :]) + nn(low, whi[:depth, :]) + nn(high, wlo[:depth, :])
+        @pl.loop(0, blocks)
+        def _(i):
+            high, low = halves(win[piece(i, step), :])
+            whi[piece(i, step), :] = high
+            wlo[piece(i, step), :] = low
+
+        @pl.loop(0, blocks)
+        def _(i):
+            at = piece(i, step)
+
+            def add(j, value):
+                high, low = halves(dinv[at, piece(j, step)])
+                left = whi[piece(j, step), :]
+                return value + nn(high, left) + nn(low, left) + nn(high, wlo[piece(j, step), :])
+
+            value = lax.fori_loop(0, i + 1, add, jnp.zeros((step, order), F32))
             high, low = halves(value)
-            mhi[at:at + step, :] = high
-            mlo[at:at + step, :] = low
+            mhi[at, :] = high
+            mlo[at, :] = low
 
     solver = (p > 0) & (q == p - 1)
 
@@ -210,7 +230,7 @@
     def line_send(k, go):
         t = k * owners + mine
 
-        @pl.when(owner)
+        @pl.when(owner & (p == k))
         def _():
             @pl.loop(0, rows - 1)
             def _(i):
@@ -219,8 +239,10 @@
                     act(remote(y_all.at[t], y_all.at[t], ln_send.at[i], y_recv.at[t], at_line(i), q), go)
 
     def has_whole(k, row, col):
-        handed = (row > k) & (col == k)
-        return handed if k == 0 else handed | ((row == k) & (col == k - 1))
+        return ((row > k) & (col == k)) | ((row == k) & (col == k - 1))
+
+    def has_made(k, row, col):
+        return (row == k) & ((k == 0) | (col == k - 1))
 
     def plane_send(k, go):
         t = k * owners + mine
@@ -237,7 +259,8 @@
 
     def solved_send(k, c, go):
         t = k * owners + c
-        if k < rows - 1:
+        @pl.when(k < rows - 1)
+        def _():
             act(remote(y_all.at[t], y_all.at[t], dx_send.at[c], y_recv.at[t], p + 1, k), go)
 
         @pl.when(c != q)
@@ -257,8 +280,8 @@
     def y_wait(t):
         remote(y_all.at[t], y_all.at[t], ln_send.at[0], y_recv.at[t], p, at_plane(0)).wait_recv()
 
-    def rhs_plane(go):
-        @pl.when(owner)
+    def rhs_plane(go, when=True):
+        @pl.when(owner & when)
         def _():
             @pl.loop(0, rows - 1)
             def _(j):
@@ -296,9 +319,7 @@
     first_send(True)
     df_send_one(True)
 
-    @pl.when(p >= 2)
-    def _():
-        rhs_plane(True)
+    rhs_plane(True, p >= 2)
 
     @pl.when(solver)
     def _():
@@ -307,79 +328,81 @@
             def _():
                 remote(usend, ubuf.at[c], df_send, df_recv.at[c], p, at_plane(0)).wait_recv()
 
-    for k in range(rows):
+    @pl.loop(0, rows)
+    def _(k):
         base = k * owners
         handed = (p > k) & (q == k)
-        made = p == k if k == 0 else (p == k) & (q == k - 1)
+        made = has_made(k, p, q)
 
         @pl.when(handed)
         def _():
-            last = order - step
-            for at in range(0, order, step):
+            def take(i):
                 for n in range(pair):
-                    c = at // tile + n
+                    c = i * pair + n
                     y_wait(base + c)
                     chain_send(k, c, True)
-                    xx[c * tile:(c + 1) * tile, :] = turned(y_all[base + c])
-                if at < last:
-                    weights = xx[at:at + step, :]
-                    value = nn(mhi[:, at:at + step], weights) + nn(mlo[:, at:at + step], weights)
-                    acc[...] = value if at == 0 else acc[...] + value
-
-            def product(at):
-                weights = xx[last:, :]
-                value = nn(mhi[at:at + step, last:], weights) + nn(mlo[at:at + step, last:], weights)
-                return acc[at:at + step, :] + value
+                    xx[piece(c, tile), :] = turned(y_all[base + c])
+
+            acc[...] = jnp.zeros_like(acc)
+
+            @pl.loop(0, blocks - 1)
+            def _(i):
+                take(i)
+                at = piece(i, step)
+                weights = xx[at, :]
+                acc[...] += nn(mhi[:, at], weights) + nn(mlo[:, at], weights)
+
+            take(blocks - 1)
+            last = order - step
 
             @pl.when(p == k + 1)
             def _():
-                for j in range(k):
+                @pl.loop(0, k)
+                def _(j):
                     @pl.loop(0, owners)
                     def _(c):
                         remote(vout.at[c], vbuf.at[j, c], v_send.at[c], v_recv.at[j, c], p, at_plane(0)).wait_recv()
-
-                for at in range(0, order, step):
-                    whole = product(at)
-                    for n in range(pair):
-                        c = at // tile + n
-                        value = ubuf[c] - fold(whole[n * tile:(n + 1) * tile])
-                        for j in range(k):
-                            value = value - vbuf[j, c]
-                        y_all[base + owners + c] = value
-                        if k < rows - 1:
-                            solved_send(k + 1, c, True)
-
-            @pl.when(p > k + 1)
-            def _():
-                for at in range(0, order, step):
-                    whole = product(at)
-                    for n in range(pair):
-                        c = at // tile + n
-                        vout[c] = fold(whole[n * tile:(n + 1) * tile])
+                        ubuf[c] = ubuf[c] - vbuf[j, c]
+
+            @pl.loop(0, blocks)
+            def _(i):
+                at = piece(i, step)
+                weights = xx[last:, :]
+                whole = acc[at, :] + nn(mhi[at, last:], weights) + nn(mlo[at, last:], weights)
+                for n in range(pair):
+                    c = i * pair + n
+                    value = fold(whole[n * tile:(n + 1) * tile])
+
+                    @pl.when(p == k + 1)
+                    def _():
+                        y_all[base + owners + c] = ubuf[c] - value
+                        solved_send(k + 1, c, True)
+
+                    @pl.when(p > k + 1)
+                    def _():
+                        vout[c] = value
                         v_send_one(k, c, True)
 
         @pl.when(owner & jnp.logical_not(made | handed))
         def _():
             y_wait(base + mine)
 
-        @pl.when(p == k)
-        def _():
-            line_send(k, True)
+        line_send(k, True)
 
         plane_send(k, True)
 
-        @pl.when((p == k) & (p < 2))
-        def _():
-            rhs_plane(True)
+        rhs_plane(True, (p == k) & (p < 2))
 
     load_force.wait()
     for t in range(tpd):
-        for n in range(nnb):
+        @pl.loop(0, nnb)
+        def _(n):
             high, low = halves(force[t, n])
-            fhi[t, :, n * tile:(n + 1) * tile] = high
-            flo[t, :, n * tile:(n + 1) * tile] = low
-
-    for k in range(rows):
+            fhi[t, :, piece(n, tile)] = high
+            flo[t, :, piece(n, tile)] = low
+
+    @pl.loop(0, rows)
+    def _(k):
         @pl.when(jnp.logical_not(has_whole(k, p, q)))
         def _():
             @pl.loop(0, cols - 1)
@@ -423,17 +446,15 @@
     first_send(False)
     df_send_one(False)
     rhs_plane(False)
-    for k in range(rows):
-        @pl.when(p == k)
-        def _():
-            line_send(k, False)
-
-        if k > 0:
-            @pl.when((p == k) & (q == k - 1))
-            def _():
-                @pl.loop(0, owners)
-                def _(c):
-                    solved_send(k, c, False)
+    @pl.loop(0, rows)
+    def _(k):
+        line_send(k, False)
+
+        @pl.when((p == k) & (q == k - 1))
+        def _():
+            @pl.loop(0, owners)
+            def _(c):
+                solved_send(k, c, False)
 
         @pl.when((p > k) & (q == k))
         def _():

time: 61.8 us -> 66.3 us (1.073)
  Pallas kernels: 57.8 us -> 62.3 us
    pallas_call x1, Pallas kernels: 57.8 us -> 62.3 us  [per_device(): pl.pallas_call(functools.partial(kernel, rows, cols, owners, tile, nrhs,...]
where the time goes in v6:
time: 66.3 us; the launch traced here: 66.1 us
  Pallas kernels  62.3 us (94%)
  local copies, waits for them, and re-layouts  3.14 us (5%)
    pallas_call x1, Pallas kernels, per_device(): pl.pallas_call(functools.partial(kernel, rows, cols, owners, tile, nrhs,...  62.3 us
    unnamed x2, local copies, waits for them, and re-layouts  3.14 us

profile of v6, /device:TPU:0, one launch (start us, length us, event | category | flops | bytes accessed | tf_op | source)
XLA Modules:
  0.0 66.1 jit_solution(3656547886541720360)
XLA Ops:
  0.6 62.3 %shard_map.95 = (f32[64,1024]{1,0:T(8,128)}, f32[1,2,64,128]{3,2,1,0:T(8,128)}) custom-call(f32[64,1024]{1,0:T(8,128)} %rhs_hbm.1, f32[64,2048]{1,0:T(8,128)} %psol_hbm.1, f32[1024,2048]{1,0:T(8,128)} %panel_hbm.1, f32[1,1024,1,1024]{3,2,1,0:T(1,128)} %win_hbm.1, f32[1,1024,1024]{2,1,0:T(8,128)} %dinv_hbm.1, s32[1,2]{1,0:T(1,128)} %tlist_hbm.1, ...), custom_call_target="tpu_custom_call" | custom-call | tf_op jit(solution)/shard_map/pallas_call | solution.py:481
  62.9 1.7 %copy.12 = f32[64,1024]{1,0:T(8,128)} copy(f32[64,1024]{1,0:T(8,128)} %get-tuple-element.4) | data formatting | bytes 524288
  64.6 1.5 %copy.13 = f32[1,2,64,128]{3,2,1,0:T(8,128)} copy(f32[1,2,64,128]{3,2,1,0:T(8,128)} %get-tuple-element.5) | data formatting | bytes 131072

commit v7 on v4

--- a/solution.py
+++ b/solution.py
@@ -32,7 +32,7 @@
     sol_out, res_out,
     tlist, nlist, psol, panel, win, dinv, force, xpast, xx, whi, wlo, mhi, mlo, fhi, flo, acc,
     part, rs_buf, outp, usend, ubuf, vout, vbuf, y_all, rhs_all,
-    load_sem, panel_sem, rhs_sem,
+    out_sem, load_sem, panel_sem, rhs_sem,
     rs_send, rs_recv, df_send, df_recv, dx_send, ch_send, sc_send, ln_send, ag_send, y_recv,
     rl_send, ra_send, r_recv, v_send, v_recv,
 ):
@@ -137,16 +137,14 @@
     step = min(256, order)
     pair = step // tile
 
-    @pl.loop(0, order // step)
-    def _(i):
+    for i in range(order // step):
         for n in range(pair):
             panel_copy(i * pair + n).wait()
 
-        @pl.when(i == max(order // step // 2 - 1, 0))
-        def _():
+        if i == max(order // step // 2 - 1, 0):
             load_dinv.start()
 
-        high, low = halves(panel[pl.ds(pl.multiple_of(i * step, step), step), :])
+        high, low = halves(panel[i * step:(i + 1) * step, :])
         weights = xpast[...]
         value = nn(high, weights) + nn(low, weights)
         for n in range(pair):
@@ -390,8 +388,13 @@
                 def _():
                     y_wait(k * owners + c)
 
+    def sol_copy(c):
+        return pltpu.make_async_copy(
+            y_all.at[p * owners + c], sol_out.at[:, c * tile:(c + 1) * tile], out_sem.at[c]
+        )
+
     for c in range(owners):
-        sol_out[:, c * tile:(c + 1) * tile] = y_all[p * owners + c]
+        sol_copy(c).start()
 
     load_tlist.wait()
     load_nlist.wait()
@@ -411,6 +414,9 @@
         weights = jnp.concatenate([turned(y_all[nlist[0, t, n]]) for n in range(nnb)], axis=0)
         term = fold(nn(fhi[t], weights) + nn(flo[t], weights))
         res_out[0, t] = rhs_all[tlist[0, t]] - term
+
+    for c in range(owners):
+        sol_copy(c).wait()
 
     rhs_line(False)
 
@@ -464,7 +470,7 @@
             jax.ShapeDtypeStruct((1, tpd, nrhs, tile), F32),
         ),
         in_specs=[hbm] * 8,
-        out_specs=(vmem, vmem),
+        out_specs=(hbm, vmem),
         scratch_shapes=[
             pltpu.SMEM((1, tpd), jnp.int32),
             pltpu.SMEM((1, tpd, nnb), jnp.int32),
@@ -491,6 +497,7 @@
             pltpu.VMEM((max(rows - 2, 1), owners, nrhs, tile), F32),
             pltpu.VMEM((tiles, nrhs, tile), F32),
             pltpu.VMEM((tiles, nrhs, tile), F32),
+            dma((owners,)),
             dma((6,)),
             dma((owners,)),
             dma((owners,)),

time: 61.8 us -> 61.8 us (level)
  no operation moved by 1% of the time
where the time goes in v7:
time: 61.8 us; the launch traced here: 61.6 us
  Pallas kernels  57.8 us (94%)
  local copies, waits for them, and re-layouts  3.14 us (5%)
  between operations  0.64 us (1%)
    pallas_call x1, Pallas kernels, per_device(): pl.pallas_call(functools.partial(kernel, rows, cols, owners, tile, nrhs,...  57.8 us
    unnamed x2, local copies, waits for them, and re-layouts  3.14 us

profile of v7, /device:TPU:0, one launch (start us, length us, event | category | flops | bytes accessed | tf_op | source)
XLA Modules:
  0.0 61.6 jit_solution(10354050251622719454)
XLA Ops:
  0.6 57.8 %shard_map.95 = (f32[64,1024]{1,0:T(8,128)}, f32[1,2,64,128]{3,2,1,0:T(8,128)}) custom-call(f32[64,1024]{1,0:T(8,128)} %rhs_hbm.1, f32[64,2048]{1,0:T(8,128)} %psol_hbm.1, f32[1024,2048]{1,0:T(8,128)} %panel_hbm.1, f32[1,1024,1,1024]{3,2,1,0:T(1,128)} %win_hbm.1, f32[1,1024,1024]{2,1,0:T(8,128)} %dinv_hbm.1, s32[1,2]{1,0:T(1,128)} %tlist_hbm.1, ...), custom_call_target="tpu_custom_call" | custom-call | tf_op jit(solution)/shard_map/pallas_call | solution.py:466
  58.4 1.7 %copy.12 = f32[64,1024]{1,0:T(8,128)} copy(f32[64,1024]{1,0:T(8,128)} %get-tuple-element.4) | data formatting | bytes 524288
  60.1 1.5 %copy.13 = f32[1,2,64,128]{3,2,1,0:T(8,128)} copy(f32[1,2,64,128]{3,2,1,0:T(8,128)} %get-tuple-element.5) | data formatting | bytes 131072
